TPU v7x, 32 devices: a whole 2x2x4 slice. The times are simulated.
32 devices in a mesh: dp: 16 (over z, y, x), mp: 2 (over core).
Axes of the slice: x: 2, y: 2, z: 4, core: 2. Of those that a mesh axis runs over, the one named last changes fastest.
Arguments:
- inputs: bfloat16 [8192, 3072], P('dp', 'mp'), may hold values from -6 to 6
- queries: bfloat16 [8192, 3072], P('dp', 'mp'), may hold values from -5 to 5
- keys: bfloat16 [8192, 3072], P('dp', 'mp'), may hold values from -5 to 5
- values: bfloat16 [8192, 3072], P('dp', 'mp'), may hold values from -16 to 16
- out_weight: bfloat16 [3072, 3072], P('dp', 'mp'), may hold values from -0.109375 to 0.109375
Outputs:
- block_out: bfloat16 [8192, 3072], P('dp', 'mp')
All inputs are finite; a program needn't handle non-finite values.
Results may differ from a plain program's by a relative error of at most 0.0034.
Values may be sent and summed in bfloat16 or wider, within the bound.
A program may use at most 64 MiB of HBM per device.

v0:
```python
import math

import jax
import jax.numpy as jnp
from jax import lax
from jax.sharding import PartitionSpec as P

HEAD_DIM = 128
PATCHES = 256


def shards(inputs, queries, keys, values, out_weight):
    tok_rows, local_width = queries.shape
    head_count = local_width // HEAD_DIM
    images = tok_rows // PATCHES
    split_shape = (images, PATCHES, head_count, HEAD_DIM)
    scores = jnp.einsum(
        "bqhd,bkhd->bhqk",
        queries.reshape(split_shape),
        keys.reshape(split_shape),
        preferred_element_type=jnp.float32,
    ) / math.sqrt(HEAD_DIM)
    row_max = jnp.max(scores, axis=-1, keepdims=True)
    shifted = jnp.exp(scores - row_max)
    probs = (shifted / jnp.sum(shifted, axis=-1, keepdims=True)).astype(jnp.bfloat16)
    attended = jnp.einsum(
        "bhqk,bkhd->bqhd", probs, values.reshape(split_shape), preferred_element_type=jnp.float32
    )
    attended = attended.astype(jnp.bfloat16).reshape(tok_rows, local_width)
    all_heads = lax.all_gather(attended, "mp", axis=1, tiled=True)
    gathered = lax.all_gather(out_weight, "dp", axis=0, tiled=True)
    projected = jnp.dot(all_heads, gathered, preferred_element_type=jnp.float32)
    return (inputs.astype(jnp.float32) + projected).astype(jnp.bfloat16)


def solution(mesh):
    return jax.shard_map(
        shards,
        mesh=mesh,
        in_specs=(P("dp", "mp"), P("dp", "mp"), P("dp", "mp"), P("dp", "mp"), P("dp", "mp")),
        out_specs=P("dp", "mp"),
        check_vma=False,
    )
```

profile of v0, /device:TPU:0, one launch (start us, length us, event | category | flops | bytes accessed | tf_op | source)
XLA Modules:
  0.0 192.1 jit_solution(12400219498978801608)
XLA Ops:
  6.5 0.0 all-gather.3.cloned.1.call-start
  6.5 2.9 %reshape.18 = bf16[2,256,12,128]{3,2,1,0:T(8,128)(2,1)S(1)} reshape(bf16[512,1536]{1,0:T(8,128)(2,1)} %param.6) | data formatting | bytes 3145728 | tf_op jit(solution)/shard_map/reshape | solution.py:19
  9.4 4.0 %reshape.19 = bf16[2,256,12,128]{3,2,1,0:T(8,128)(2,1)} reshape(bf16[512,1536]{1,0:T(8,128)(2,1)} %param.7) | data formatting | bytes 3145728 | tf_op jit(solution)/shard_map/reshape | solution.py:20
  13.4 2.6 %fusion.9 = f32[2,12,256,256]{2,3,1,0:T(8,128)S(1)} fusion(bf16[2,256,12,128]{3,2,1,0:T(8,128)(2,1)} %reshape.19, bf16[2,256,12,128]{3,2,1,0:T(8,128)(2,1)S(1)} %reshape.18), kind=kOutput, calls=%fused_computation.11 | convolution fusion | flops 402653184 | bytes 9437184 | tf_op jit(solution)/shard_map/bqhd,bkhd->bhqk/dot_general | solution.py:17
  16.0 4.3 %fusion.16 = (f32[2,12,256]{2,1,0:T(8,128)S(1)}, f32[2,12,256,256]{2,3,1,0:T(8,128)}) fusion(f32[2,12,256,256]{2,3,1,0:T(8,128)S(1)} %fusion.9), kind=kOutput, calls=%fused_computation.16 | output fusion | flops 6291711 | bytes 12607488 | tf_op jit(solution)/shard_map/sub | solution.py:24
  20.3 2.9 %reshape.20 = bf16[2,256,12,128]{3,2,1,0:T(8,128)(2,1)S(1)} reshape(bf16[512,1536]{1,0:T(8,128)(2,1)} %param.8) | data formatting | bytes 3145728 | tf_op jit(solution)/shard_map/reshape | solution.py:27
  23.2 5.2 %fusion.12 = bf16[2,256,12,128]{3,1,2,0:T(8,128)(2,1)} fusion(bf16[2,256,12,128]{3,2,1,0:T(8,128)(2,1)S(1)} %reshape.20, f32[2,12,256,256]{2,3,1,0:T(8,128)} %get-tuple-element.6, f32[2,12,256]{2,1,0:T(8,128)S(1)} %get-tuple-element.5), kind=kOutput, calls=%fused_computation.14 | convolution fusion | flops 406585344 | bytes 9461760 | tf_op jit(solution)/shard_map/bhqk,bkhd->bqhd/dot_general | solution.py:26
  28.4 3.7 %copy.17 = bf16[2,256,12,128]{1,0,3,2:T(2,128)(2,1)S(1)} copy(bf16[2,256,12,128]{3,1,2,0:T(8,128)(2,1)} %fusion.12) | data formatting | bytes 3145728 | tf_op jit(solution)/shard_map/convert_element_type | solution.py:29
  32.1 0.0 copy-start
  32.1 1.5 copy.25
  33.5 0.0 all-gather.3.cloned.1.call-update
  33.6 0.0 all-gather.5.cloned.1.call-start
  33.6 0.7 all-gather.5.cloned.1.call-update
  34.3 14.2 %all-gather.3.cloned.1.call-done = bf16[512,3072]{0,1:T(8,128)(2,1)} async-done(((bf16[512,1536]{0,1:T(8,128)(2,1)}), bf16[512,3072]{0,1:T(8,128)(2,1)}) %all-gather.3.cloned.1.call-update) | async-done | bytes 3145744 | tf_op jit(solution)/shard_map/all_gather | solution.py:30
  48.6 126.5 %all-gather.5.cloned.1.call-done = bf16[3072,1536]{1,0:T(8,128)(2,1)} async-done(((bf16[192,1536]{1,0:T(8,128)(2,1)}), bf16[3072,1536]{1,0:T(8,128)(2,1)}) %all-gather.5.cloned.1.call-update) | async-done | bytes 9437200 | tf_op jit(solution)/shard_map/all_gather | solution.py:31
  175.0 0.0 copy-done
  175.0 10.3 %fusion.6 = bf16[512,1536]{1,0:T(8,128)(2,1)} fusion(bf16[512,3072]{0,1:T(8,128)(2,1)} %all-gather.3.cloned.1.call-done, bf16[3072,1536]{1,0:T(8,128)(2,1)} %all-gather.5.cloned.1.call-done, bf16[512,1536]{1,0:T(8,128)(2,1)S(1)} %copy-done), kind=kOutput, calls=%fused_computation.8 | convolution fusion | flops 4834197504 | bytes 15728640 | tf_op jit(solution)/shard_map/dot_general | solution.py:32
Async XLA Ops:
  6.5 42.0 %all-gather.3.cloned.1.call-start = ((), (), s32[]{:S(2)}) async-start(), calls=%async_computation | async-start | bytes 4718592 | tf_op jit(solution)/shard_map/all_gather | solution.py:30
  32.1 143.0 %copy-start = (bf16[512,1536]{1,0:T(8,128)(2,1)S(1)}, bf16[512,1536]{1,0:T(8,128)(2,1)}, u32[]{:S(2)}) copy-start(bf16[512,1536]{1,0:T(8,128)(2,1)} %param.5) | copy-start | bytes 4718596
  33.6 141.4 %all-gather.5.cloned.1.call-start = ((), (), s32[]{:S(2)}) async-start(), calls=%async_computation.1 | async-start | bytes 10027008 | tf_op jit(solution)/shard_map/all_gather | solution.py:31
Sparse Core Ops, SparseCore 0:
  33.7 14.8 all-gather.2
  51.3 123.6 all-gather.4
where the time goes:
time: 193 us; the launch traced here: 192 us
  waiting for transfers between devices  141 us (73%)
  matrix products  18.1 us (9%)
  local copies, waits for them, and re-layouts  14.9 us (8%)
  between operations  13.4 us (7%)
  other arithmetic  4.27 us (2%)
    all_gather x1, waiting for transfers between devices, shards(): gathered = lax.all_gather(out_weight, 'dp', axis=0, tiled=True)  126 us
    all_gather x1, waiting for transfers between devices, shards(): all_heads = lax.all_gather(attended, 'mp', axis=1, tiled=True)  14.2 us
    dot_general x1, matrix products, shards(): projected = jnp.dot(all_heads, gathered, preferred_element_type=jnp.float32)  10.3 us
    dot_general x1, matrix products, shards(): jnp.einsum('bhqk,bkhd->bqhd', probs, values.reshape(split_shape), preferr...  5.19 us
    sub x1, other arithmetic, shards(): shifted = jnp.exp(scores - row_max)  4.27 us
    reshape x1, local copies, waits for them, and re-layouts, shards(): keys.reshape(split_shape)  3.97 us
  transfers between devices with their start and end apart: 2, of which 2 were waited for; matrix products, arithmetic and copies ran while one was open for 0% of the time, Pallas kernels for 0%

commit v1 on v0

v1 whole, which is shorter than its diff:
```python
import functools
import math

import jax
import jax.numpy as jnp
from jax import lax
from jax.experimental import pallas as pl
from jax.experimental.pallas import tpu as pltpu
from jax.sharding import PartitionSpec as P

HEAD_DIM = 128
PATCHES = 256
MESH = pl.DeviceIdType.MESH

PARTS = (("zxy", 0, 1), ("zyx", 1, 1), ("xzy", 2, 2), ("yzx", 4, 2))
GROUPS = 12
HEAD_START = 4


def hops(order, rx, ry, dz):
    diff = {"x": rx, "y": ry, "z": dz}
    last = max([i for i in range(3) if diff[order[i]]], default=-1)
    out = []
    if last >= 0 and order[last] == "z":
        out.append("u" if dz < 0 else "d")
    for axis in order[last + 1:]:
        out.extend(("u", "d") if axis == "z" else (axis,))
    return out


def arrivals(deep):
    chips = [(x, y, z) for z in range(deep) for y in range(2) for x in range(2)]
    ready, busy, when = [], {}, {}
    for c in chips:
        for rank, p in enumerate(range(len(PARTS))):
            ready.append((0.0, rank, c, p, c))
    while ready:
        ready.sort()
        now, rank, c, p, s = ready.pop(0)
        order, _, size = PARTS[p]
        rx, ry, dz = c[0] ^ s[0], c[1] ^ s[1], s[2] - c[2]
        if c != s:
            when.setdefault((p, rx, ry, dz), []).append(now)
        for hop in hops(order, rx, ry, dz):
            to = {
                "x": (1 - c[0], c[1], c[2]), "y": (c[0], 1 - c[1], c[2]),
                "u": (c[0], c[1], c[2] + 1), "d": (c[0], c[1], c[2] - 1),
            }[hop]
            if 0 <= to[2] < deep:
                end = max(now, busy.get((c, hop), 0.0)) + size
                busy[(c, hop)] = end
                ready.append((end + 0.3, rank, to, p, s))
    return sorted(when, key=lambda e: (sum(when[e]) / len(when[e]), e))


def kernel(deep, x_hbm, q_hbm, k_hbm, v_hbm, w_hbm, o_hbm,
           wbuf, xin, qv, kv, vv, att, acc, obuf,
           recv, sent, local, att_sent, att_recv):
    me, half = lax.axis_index("dp"), lax.axis_index("mp")
    x, y, z = me % 2, (me // 2) % 2, me // 4
    rows, width = w_hbm.shape
    tokens = q_hbm.shape[0]
    images, heads = tokens // PATCHES, width // HEAD_DIM
    sixth = rows // 6

    def index_of(cx, cy, cz):
        return (cz * 2 + cy) * 2 + cx

    near = {
        "x": index_of(1 - x, y, z), "y": index_of(x, 1 - y, z),
        "u": index_of(x, y, z + 1), "d": index_of(x, y, z - 1),
    }
    open_way = {"x": None, "y": None, "u": z < deep - 1, "d": z > 0}
    lane = {"x": 0, "y": 1, "u": 2, "d": 3}

    def maybe(cond, fn):
        if cond is None:
            fn()
        else:
            pl.when(cond)(fn)

    loads = [
        pltpu.make_async_copy(a, b, local.at[i])
        for i, (a, b) in enumerate(((q_hbm, qv), (k_hbm, kv), (v_hbm, vv), (x_hbm, xin)))
    ]
    own = pl.ds(pl.multiple_of(me * rows, 16), rows)
    loads.append(pltpu.make_async_copy(w_hbm, wbuf.at[own], local.at[4]))
    for load in loads:
        load.start()

    barrier = pltpu.get_barrier_semaphore()
    pl.semaphore_signal(barrier, inc=1, device_id=(me, 1 - half), device_id_type=MESH)
    for hop in "xyud":
        def greet(hop=hop):
            pl.semaphore_signal(barrier, inc=1, device_id=(near[hop], half), device_id_type=MESH)
        maybe(open_way[hop], greet)
    pl.semaphore_wait(barrier, 3 + jnp.minimum(z, 1) + jnp.minimum(deep - 1 - z, 1))

    def piece(p, source):
        _, first, size = PARTS[p]
        return wbuf.at[pl.ds(pl.multiple_of(source * rows + first * sixth, 16), size * sixth)]

    def copy(p, source, hop, src=None):
        spot = piece(p, source)
        return pltpu.make_async_remote_copy(
            src_ref=spot if src is None else src,
            dst_ref=spot,
            send_sem=sent.at[lane[hop]],
            recv_sem=recv.at[p, source],
            device_id=(near[hop], half),
            device_id_type=MESH,
        )

    first_sends = []
    for p, (order, first, size) in enumerate(PARTS):
        for hop in hops(order, 0, 0, 0):
            axis = "z" if hop in "ud" else hop
            first_sends.append((order.index(axis), p, hop))
    for _, p, hop in sorted(first_sends):
        _, first, size = PARTS[p]
        src = w_hbm.at[pl.ds(first * sixth, size * sixth)]
        maybe(open_way[hop], lambda p=p, hop=hop, src=src: copy(p, me, hop, src).start())

    def event(p, rx, ry, dz):
        source = index_of((x + rx) % 2, (y + ry) % 2, z + dz)

        def handle():
            copy(p, source, "x").wait_recv()
            for hop in hops(PARTS[p][0], rx, ry, dz):
                maybe(open_way[hop], lambda hop=hop: copy(p, source, hop).start())

        cond = None if dz == 0 else (z + dz < deep if dz > 0 else z + dz >= 0)
        maybe(cond, handle)

    def attend(unit):
        r = pl.multiple_of((unit // heads) * PATCHES, PATCHES)
        c = pl.multiple_of((unit % heads) * HEAD_DIM, HEAD_DIM)
        here = (pl.ds(r, PATCHES), pl.ds(c, HEAD_DIM))
        s = lax.dot_general(qv[here], kv[here], (((1,), (1,)), ((), ())), preferred_element_type=jnp.float32)
        s = s * (1.0 / math.sqrt(HEAD_DIM))
        e = jnp.exp(s - jnp.max(s, axis=-1, keepdims=True))
        probs = (e / jnp.sum(e, axis=-1, keepdims=True)).astype(jnp.bfloat16)
        a = jnp.dot(probs, vv[here], preferred_element_type=jnp.float32)
        att[pl.ds(r, PATCHES), pl.ds(pl.multiple_of(half * width + c, HEAD_DIM), HEAD_DIM)] = a.astype(jnp.bfloat16)

    def share(image):
        spot = att.at[pl.ds(image * PATCHES, PATCHES), pl.ds(pl.multiple_of(half * width, HEAD_DIM), width)]
        return pltpu.make_async_remote_copy(
            src_ref=spot, dst_ref=spot, send_sem=att_sent.at[image], recv_sem=att_recv.at[image],
            device_id=(me, 1 - half), device_id_type=MESH,
        )

    block, tile = 4 * rows, 256

    def project(dz):
        depth = pl.ds(pl.multiple_of((z + dz) * block, HEAD_DIM), block)

        def run():
            @pl.loop(0, width // tile)
            def _(i):
                cols = pl.ds(pl.multiple_of(i * tile, tile), tile)
                start = xin[:, cols].astype(jnp.float32) if dz == 0 else acc[:, cols]
                acc[:, cols] = start + jnp.dot(att[:, depth], wbuf[depth, cols], preferred_element_type=jnp.float32)

        maybe(None if dz == 0 else (z + dz < deep if dz > 0 else z + dz >= 0), run)

    order = arrivals(deep)
    for load in loads[:3]:
        load.wait()

    units = images * heads
    step = units // GROUPS
    early = 2 * len(order) // 3
    done = 0
    shared = 0
    for g in range(GROUPS):
        pl.loop(g * step, (g + 1) * step)(attend)
        while shared < images and (g + 1) * step >= (shared + 1) * heads:
            share(shared).start()
            shared += 1
        if g + 1 > HEAD_START:
            upto = early * (g + 1 - HEAD_START) // (GROUPS - HEAD_START)
            for e in order[done:upto]:
                event(*e)
            done = upto
    for load in loads[3:]:
        load.wait()
    for image in range(images):
        share(image).wait_recv()

    left = {}
    for e in order[done:]:
        left[e[3]] = left.get(e[3], 0) + 1
    for dz in sorted({e[3] for e in order}, key=lambda d: (abs(d), d)):
        if dz not in left:
            project(dz)
    for e in order[done:]:
        event(*e)
        left[e[3]] -= 1
        if left[e[3]] == 0:
            project(e[3])

    outs = []
    for i in range(width // tile):
        cols = pl.ds(i * tile, tile)
        obuf[:, cols] = acc[:, cols].astype(jnp.bfloat16)
        out = pltpu.make_async_copy(obuf.at[:, cols], o_hbm.at[:, cols], local.at[5 + i])
        out.start()
        outs.append(out)

    def drain(hop, count):
        spot = wbuf.at[pl.ds(0, count)]
        pltpu.make_async_remote_copy(
            src_ref=spot, dst_ref=spot, send_sem=sent.at[lane[hop]], recv_sem=recv.at[0, 0],
            device_id=(near[hop], half), device_id_type=MESH,
        ).wait_send()

    carried = {hop: {} for hop in "xyud"}
    for p, (name, _, size) in enumerate(PARTS):
        for at in range(deep):
            for rx in range(2):
                for ry in range(2):
                    for dz in range(-at, deep - at):
                        for hop in hops(name, rx, ry, dz):
                            if (hop == "u" and at == deep - 1) or (hop == "d" and at == 0):
                                continue
                            carried[hop][at] = carried[hop].get(at, 0) + size * sixth
    for hop in "xyud":
        for at, count in carried[hop].items():
            pl.when(z == at)(functools.partial(drain, hop, count))
    for image in range(images):
        share(image).wait_send()
    for out in outs:
        out.wait()


def fused(deep, inputs, queries, keys, values, out_weight):
    tokens, width = queries.shape
    rows = out_weight.shape[0]
    whole = 4 * deep * rows
    bf16, f32 = jnp.bfloat16, jnp.float32
    return pl.pallas_call(
        functools.partial(kernel, deep),
        out_shape=jax.ShapeDtypeStruct((tokens, width), bf16),
        in_specs=[pl.BlockSpec(memory_space=pl.ANY)] * 5,
        out_specs=pl.BlockSpec(memory_space=pl.ANY),
        scratch_shapes=[
            pltpu.VMEM((whole, width), bf16),
            pltpu.VMEM((tokens, width), bf16),
            pltpu.VMEM((tokens, width), bf16),
            pltpu.VMEM((tokens, width), bf16),
            pltpu.VMEM((tokens, width), bf16),
            pltpu.VMEM((tokens, whole), bf16),
            pltpu.VMEM((tokens, width), f32),
            pltpu.VMEM((tokens, width), bf16),
            pltpu.SemaphoreType.DMA((len(PARTS), 4 * deep)),
            pltpu.SemaphoreType.DMA((4,)),
            pltpu.SemaphoreType.DMA((5 + width // 256,)),
            pltpu.SemaphoreType.DMA((tokens // PATCHES,)),
            pltpu.SemaphoreType.DMA((tokens // PATCHES,)),
        ],
        compiler_params=pltpu.CompilerParams(
            collective_id=0, has_side_effects=True, vmem_limit_bytes=48 * 1024 * 1024
        ),
    )(inputs, queries, keys, values, out_weight)


def general(inputs, queries, keys, values, out_weight):
    tok_rows, local_width = queries.shape
    head_count = local_width // HEAD_DIM
    images = tok_rows // PATCHES
    split_shape = (images, PATCHES, head_count, HEAD_DIM)
    gathered = lax.all_gather(out_weight, "dp", axis=0, tiled=True)
    scores = jnp.einsum(
        "bqhd,bkhd->bhqk",
        queries.reshape(split_shape),
        keys.reshape(split_shape),
        preferred_element_type=jnp.float32,
    ) / math.sqrt(HEAD_DIM)
    row_max = jnp.max(scores, axis=-1, keepdims=True)
    shifted = jnp.exp(scores - row_max)
    probs = (shifted / jnp.sum(shifted, axis=-1, keepdims=True)).astype(jnp.bfloat16)
    attended = jnp.einsum(
        "bhqk,bkhd->bqhd", probs, values.reshape(split_shape), preferred_element_type=jnp.float32
    )
    attended = attended.astype(jnp.bfloat16).reshape(tok_rows, local_width)
    all_heads = lax.all_gather(attended, "mp", axis=1, tiled=True)
    projected = jnp.dot(all_heads, gathered, preferred_element_type=jnp.float32)
    return (inputs.astype(jnp.float32) + projected).astype(jnp.bfloat16)


def solution(mesh):
    parts, halves = mesh.shape["dp"], mesh.shape["mp"]

    def shards(inputs, queries, keys, values, out_weight):
        rows, width = out_weight.shape
        tokens = queries.shape[0]
        if (parts % 4 == 0 and 4 < parts <= 32 and halves == 2 and rows % 96 == 0 and width % 256 == 0
                and (tokens // PATCHES) * (width // HEAD_DIM) % GROUPS == 0):
            return fused(parts // 4, inputs, queries, keys, values, out_weight)
        return general(inputs, queries, keys, values, out_weight)

    return jax.shard_map(
        shards,
        mesh=mesh,
        in_specs=(P("dp", "mp"),) * 5,
        out_specs=P("dp", "mp"),
        check_vma=False,
    )
```

time: 193 us -> 87 us (0.45)
  waiting for transfers between devices: 141 us -> 0 us
  Pallas kernels: 0 us -> 81.8 us
  matrix products: 18.1 us -> 0 us
  between operations: 13.4 us -> 0.01 us
  local copies, waits for them, and re-layouts: 14.9 us -> 5.02 us
  other arithmetic: 4.27 us -> 0 us
    all_gather x2 -> x0, waiting for transfers between devices: 141 us -> none  [the longest x1 126 us: shards(): gathered = lax.all_gather(out_weight, 'dp', axis=0, tiled=True)]
    pallas_call x0 -> x1, Pallas kernels: none -> 81.8 us  [fused(): pl.pallas_call(functools.partial(kernel, deep), out_shape=jax.ShapeDtypeS...]
    dot_general x3 -> x0, matrix products: 18.1 us -> none  [the longest x1 10.3 us: shards(): projected = jnp.dot(all_heads, gathered, preferred_element_type=jnp.float32)]
    reshape x3 -> x0, local copies, waits for them, and re-layouts: 9.75 us -> none  [the longest x1 3.97 us: shards(): keys.reshape(split_shape)]
    sub x1 -> x0, other arithmetic: 4.27 us -> none  [shards(): shifted = jnp.exp(scores - row_max)]
    convert_element_type x1 -> x0, local copies, waits for them, and re-layouts: 3.69 us -> none  [shards(): attended = attended.astype(jnp.bfloat16).reshape(tok_rows, local_width)]
    unnamed x3 -> x7, local copies, waits for them, and re-layouts: 1.49 us -> 5.02 us
  transfers between devices with their start and end apart: 2 -> 0, of which waited for: 2 -> 0; matrix products, arithmetic and copies ran while one was open for 0% -> 0% of each run, Pallas kernels for 0% -> 0%
where the time goes in v1:
time: 87 us; the launch traced here: 86.8 us
  Pallas kernels  81.8 us (94%)
  local copies, waits for them, and re-layouts  5.02 us (6%)
    pallas_call x1, Pallas kernels, fused(): pl.pallas_call(functools.partial(kernel, deep), out_shape=jax.ShapeDtypeS...  81.8 us
    unnamed x7, local copies, waits for them, and re-layouts  5.02 us

profile of v1, /device:TPU:0, one launch (start us, length us, event | category | flops | bytes accessed | tf_op | source)
XLA Modules:
  0.0 86.8 jit_solution(17086927323194000019)
XLA Ops:
  0.0 0.0 copy-start
  0.0 1.4 %copy-done = bf16[512,1536]{1,0:T(8,128)(2,1)S(1)} copy-done((bf16[512,1536]{1,0:T(8,128)(2,1)S(1)}, bf16[512,1536]{1,0:T(8,128)(2,1)}, u32[]{:S(2)}) %copy-start) | copy-done | bytes 1572888
  1.4 0.0 copy-start.1
  1.4 1.4 %copy-done.1 = bf16[512,1536]{1,0:T(8,128)(2,1)S(1)} copy-done((bf16[512,1536]{1,0:T(8,128)(2,1)S(1)}, bf16[512,1536]{1,0:T(8,128)(2,1)}, u32[]{:S(2)}) %copy-start.1) | copy-done | bytes 1572888
  2.8 0.0 copy-start.2
  2.8 1.1 %copy-done.2 = bf16[192,1536]{1,0:T(8,128)(2,1)S(1)} copy-done((bf16[192,1536]{1,0:T(8,128)(2,1)S(1)}, bf16[192,1536]{1,0:T(8,128)(2,1)}, u32[]{:S(2)}) %copy-start.2) | copy-done | bytes 589848
  3.9 81.8 %shard_map.55 = bf16[512,1536]{1,0:T(8,128)(2,1)S(1)} custom-call(bf16[512,1536]{1,0:T(8,128)(2,1)S(1)} %copy-done, bf16[512,1536]{1,0:T(8,128)(2,1)S(1)} %copy-done.1, bf16[512,1536]{1,0:T(8,128)(2,1)} %k_hbm.1, bf16[512,1536]{1,0:T(8,128)(2,1)} %v_hbm.1, bf16[192,1536]{1,0:T(8,128)(2,1)S(1)} %copy-done.2), custom_call_target="tpu_custom_call" | custom-call | tf_op jit(solution)/shard_map/pallas_call | solution.py:242
  85.7 1.1 %copy.7 = bf16[512,1536]{1,0:T(8,128)(2,1)} copy(bf16[512,1536]{1,0:T(8,128)(2,1)S(1)} %shard_map.55) | data formatting | bytes 3145728
Async XLA Ops:
  0.0 1.4 %copy-start = (bf16[512,1536]{1,0:T(8,128)(2,1)S(1)}, bf16[512,1536]{1,0:T(8,128)(2,1)}, u32[]{:S(2)}) copy-start(bf16[512,1536]{1,0:T(8,128)(2,1)} %x_hbm.1) | copy-start | bytes 4718596
  1.4 1.4 %copy-start.1 = (bf16[512,1536]{1,0:T(8,128)(2,1)S(1)}, bf16[512,1536]{1,0:T(8,128)(2,1)}, u32[]{:S(2)}) copy-start(bf16[512,1536]{1,0:T(8,128)(2,1)} %q_hbm.1) | copy-start | bytes 4718596
  2.8 1.1 %copy-start.2 = (bf16[192,1536]{1,0:T(8,128)(2,1)S(1)}, bf16[192,1536]{1,0:T(8,128)(2,1)}, u32[]{:S(2)}) copy-start(bf16[192,1536]{1,0:T(8,128)(2,1)} %w_hbm.1) | copy-start | bytes 1769476

commit v2 on v1

v2 whole, which is shorter than its diff:
```python
import functools
import math

import jax
import jax.numpy as jnp
from jax import lax
from jax.experimental import pallas as pl
from jax.experimental.pallas import tpu as pltpu
from jax.sharding import PartitionSpec as P

HEAD_DIM = 128
PATCHES = 256
MESH = pl.DeviceIdType.MESH

PARTS = (("zxy", 3), ("zyx", 3), ("xzy", 3), ("yzx", 3))
GROUPS = 12
HEAD_START = 4
EARLY = (1, 2)
OWN_LATE = 0.0


def hops(order, rx, ry, k, place, deep):
    diff = {"x": rx, "y": ry, "z": k}
    last = max([i for i in range(3) if diff[order[i]]], default=-1)
    out = []
    if last >= 0 and order[last] == "z":
        out.append("i" if k < 0 else "o")
    for axis in order[last + 1:]:
        out.extend(("i", "o") if axis == "z" else (axis,))
    return [hop for hop in out if hop != "o" or place > 0]


def arrivals(deep):
    chips = [(x, y, z) for z in range(deep) for y in range(2) for x in range(2)]
    ready, busy, when = [], {}, [{} for _ in range(deep // 2)]
    for c in chips:
        for p in range(len(PARTS)):
            ready.append((0.0, p, c, c, ""))
    while ready:
        ready.sort()
        now, p, c, s, only = ready.pop(0)
        order, size = PARTS[p]
        inward = 1 if c[2] < deep // 2 else -1
        place = min(c[2], deep - 1 - c[2])
        rx, ry, k = c[0] ^ s[0], c[1] ^ s[1], (s[2] - c[2]) * inward
        if OWN_LATE and c == s and not only:
            ready.append((OWN_LATE, p, c, s, order[2]))
        if c != s:
            when[place].setdefault((p, rx, ry, k), []).append(now)
        for hop in hops(order, rx, ry, k, place, deep):
            if OWN_LATE and c == s and (only != hop if only else hop == order[2]):
                continue
            to = {
                "x": (1 - c[0], c[1], c[2]), "y": (c[0], 1 - c[1], c[2]),
                "i": (c[0], c[1], c[2] + inward), "o": (c[0], c[1], c[2] - inward),
            }[hop]
            end = max(now, busy.get((c, hop), 0.0)) + size
            busy[(c, hop)] = end
            ready.append((end + 0.3, p, to, s, ""))
    orders = [sorted(w, key=lambda e, w=w: (sum(w[e]) / len(w[e]), e)) for w in when]
    late = [sum(sum(w[e]) / len(w[e]) < OWN_LATE for e in w) for w in when]
    return orders, late


def kernel(deep, x_hbm, q_hbm, k_hbm, v_hbm, w_hbm, o_hbm,
           wbuf, xin, qv, kv, vv, att, acc, obuf,
           recv, sent, local, att_sent, att_recv):
    me, half = lax.axis_index("dp"), lax.axis_index("mp")
    x, y, z = me % 2, (me // 2) % 2, me // 4
    rows, width = w_hbm.shape
    tokens = q_hbm.shape[0]
    images, heads = tokens // PATCHES, width // HEAD_DIM
    unit_rows = rows // 12
    firsts = [sum(size for _, size in PARTS[:p]) for p in range(len(PARTS))]
    places = deep // 2
    lower = z < places
    inward = jnp.where(lower, 1, -1)
    place = jnp.where(lower, z, deep - 1 - z)

    def index_of(cx, cy, cz):
        return (cz * 2 + cy) * 2 + cx

    near = {
        "x": index_of(1 - x, y, z), "y": index_of(x, 1 - y, z),
        "i": index_of(x, y, z + inward), "o": index_of(x, y, z - inward),
    }
    lane = {"x": 0, "y": 1, "i": 2, "o": 3}

    loads = [
        pltpu.make_async_copy(a, b, local.at[i])
        for i, (a, b) in enumerate(((q_hbm, qv), (k_hbm, kv), (v_hbm, vv), (x_hbm, xin)))
    ]
    own = pl.ds(pl.multiple_of(me * rows, 16), rows)
    loads.append(pltpu.make_async_copy(w_hbm, wbuf.at[own], local.at[4]))
    for load in loads:
        load.start()

    barrier = pltpu.get_barrier_semaphore()
    pl.semaphore_signal(barrier, inc=1, device_id=(me, 1 - half), device_id_type=MESH)
    for hop in "xyi":
        pl.semaphore_signal(barrier, inc=1, device_id=(near[hop], half), device_id_type=MESH)

    @pl.when(place > 0)
    def _():
        pl.semaphore_signal(barrier, inc=1, device_id=(near["o"], half), device_id_type=MESH)

    pl.semaphore_wait(barrier, 4 + jnp.minimum(place, 1))

    def piece(p, source):
        first = pl.multiple_of(source * rows + firsts[p] * unit_rows, 16)
        return wbuf.at[pl.ds(first, PARTS[p][1] * unit_rows)]

    def copy(p, source, hop, src=None):
        spot = piece(p, source)
        return pltpu.make_async_remote_copy(
            src_ref=spot if src is None else src,
            dst_ref=spot,
            send_sem=sent.at[lane[hop]],
            recv_sem=recv.at[p, source],
            device_id=(near[hop], half),
            device_id_type=MESH,
        )

    first_sends = []
    for p, (name, _) in enumerate(PARTS):
        for hop in hops(name, 0, 0, 0, 1, deep):
            first_sends.append((name.index("z" if hop in "io" else hop), p, hop))
    for _, p, hop in sorted(first_sends):
        src = w_hbm.at[pl.ds(firsts[p] * unit_rows, PARTS[p][1] * unit_rows)]
        send = copy(p, me, hop, src)
        if OWN_LATE and PARTS[p][0].index("z" if hop in "io" else hop) == 2:
            continue
        if hop == "o":
            pl.when(place > 0)(send.start)
        else:
            send.start()

    orders, late = arrivals(deep)
    seen = [0] * places

    def event(at, p, rx, ry, k):
        source = index_of((x + rx) % 2, (y + ry) % 2, z + inward * k)
        if OWN_LATE and seen[at] == late[at]:
            for own_p, (name, _) in enumerate(PARTS):
                copy(own_p, me, name[2]).start()
        seen[at] += 1
        copy(p, source, "x").wait_recv()
        for hop in hops(PARTS[p][0], rx, ry, k, at, deep):
            copy(p, source, hop).start()

    def attend(unit):
        r = pl.multiple_of((unit // heads) * PATCHES, PATCHES)
        c = pl.multiple_of((unit % heads) * HEAD_DIM, HEAD_DIM)
        here = (pl.ds(r, PATCHES), pl.ds(c, HEAD_DIM))
        s = lax.dot_general(qv[here], kv[here], (((1,), (1,)), ((), ())), preferred_element_type=jnp.float32)
        s = s * (1.0 / math.sqrt(HEAD_DIM))
        e = jnp.exp(s - jnp.max(s, axis=-1, keepdims=True))
        probs = (e / jnp.sum(e, axis=-1, keepdims=True)).astype(jnp.bfloat16)
        a = jnp.dot(probs, vv[here], preferred_element_type=jnp.float32)
        att[pl.ds(r, PATCHES), pl.ds(pl.multiple_of(half * width + c, HEAD_DIM), HEAD_DIM)] = a.astype(jnp.bfloat16)

    def share(image):
        spot = att.at[pl.ds(image * PATCHES, PATCHES), pl.ds(pl.multiple_of(half * width, HEAD_DIM), width)]
        return pltpu.make_async_remote_copy(
            src_ref=spot, dst_ref=spot, send_sem=att_sent.at[image], recv_sem=att_recv.at[image],
            device_id=(me, 1 - half), device_id_type=MESH,
        )

    block, tile = 4 * rows, 256

    def project(k, last):
        depth = pl.ds(pl.multiple_of((z + inward * k) * block, HEAD_DIM), block)

        @pl.loop(0, width // tile)
        def _(i):
            cols = pl.ds(pl.multiple_of(i * tile, tile), tile)
            start = xin[:, cols].astype(jnp.float32) if k == 0 else acc[:, cols]
            total = start + jnp.dot(att[:, depth], wbuf[depth, cols], preferred_element_type=jnp.float32)
            if last:
                obuf[:, cols] = total.astype(jnp.bfloat16)
                pltpu.make_async_copy(obuf.at[:, cols], o_hbm.at[:, cols], local.at[5 + i]).start()
            else:
                acc[:, cols] = total

    for load in loads[:3] + loads[4:]:
        load.wait()

    units = images * heads
    step = units // GROUPS
    early = [len(order) * EARLY[0] // EARLY[1] for order in orders]
    done = [0] * places
    shared = 0
    for g in range(GROUPS):
        pl.loop(g * step, (g + 1) * step)(attend)
        while shared < images and (g + 1) * step >= (shared + 1) * heads:
            share(shared).start()
            shared += 1
        if g + 1 > HEAD_START:
            for at in range(places):
                upto = early[at] * (g + 1 - HEAD_START) // (GROUPS - HEAD_START)

                @pl.when(place == at)
                def _(at=at, upto=upto):
                    for e in orders[at][done[at]:upto]:
                        event(at, *e)
                done[at] = upto
    loads[3].wait()
    for image in range(images):
        share(image).wait_recv()

    def finish(at):
        rest = orders[at][done[at]:]
        final = {k: max([i for i, e in enumerate(rest) if e[3] == k], default=-1) for k in {e[3] for e in orders[at]}}
        planes = sorted(final, key=lambda k: (final[k], abs(k)))
        planes.remove(0)
        planes.insert(0, 0)
        for k in planes:
            final[k] = max(final[k], final[0])
        at_event = 0
        for k in planes:
            for e in rest[at_event:final[k] + 1]:
                event(at, *e)
            at_event = max(at_event, final[k] + 1)
            project(k, k == planes[-1])

    for at in range(places):
        pl.when(place == at)(functools.partial(finish, at))

    def drain(hop, count):
        spot = wbuf.at[pl.ds(0, count)]
        pltpu.make_async_remote_copy(
            src_ref=spot, dst_ref=spot, send_sem=sent.at[lane[hop]], recv_sem=recv.at[0, 0],
            device_id=(near[hop], half), device_id_type=MESH,
        ).wait_send()

    def drain_all(at):
        carried = {}
        for p, rx, ry, k in orders[at] + [(p, 0, 0, 0) for p in range(len(PARTS))]:
            for hop in hops(PARTS[p][0], rx, ry, k, at, deep):
                carried[hop] = carried.get(hop, 0) + PARTS[p][1] * unit_rows
        for hop, count in carried.items():
            drain(hop, count)

    for at in range(places):
        pl.when(place == at)(functools.partial(drain_all, at))
    for image in range(images):
        share(image).wait_send()
    for i in range(width // tile):
        cols = pl.ds(i * tile, tile)
        pltpu.make_async_copy(obuf.at[:, cols], o_hbm.at[:, cols], local.at[5 + i]).wait()


def fused(deep, inputs, queries, keys, values, out_weight):
    tokens, width = queries.shape
    rows = out_weight.shape[0]
    whole = 4 * deep * rows
    bf16, f32 = jnp.bfloat16, jnp.float32
    return pl.pallas_call(
        functools.partial(kernel, deep),
        out_shape=jax.ShapeDtypeStruct((tokens, width), bf16),
        in_specs=[pl.BlockSpec(memory_space=pl.ANY)] * 5,
        out_specs=pl.BlockSpec(memory_space=pl.ANY),
        scratch_shapes=[
            pltpu.VMEM((whole, width), bf16),
            pltpu.VMEM((tokens, width), bf16),
            pltpu.VMEM((tokens, width), bf16),
            pltpu.VMEM((tokens, width), bf16),
            pltpu.VMEM((tokens, width), bf16),
            pltpu.VMEM((tokens, whole), bf16),
            pltpu.VMEM((tokens, width), f32),
            pltpu.VMEM((tokens, width), bf16),
            pltpu.SemaphoreType.DMA((len(PARTS), 4 * deep)),
            pltpu.SemaphoreType.DMA((4,)),
            pltpu.SemaphoreType.DMA((5 + width // 256,)),
            pltpu.SemaphoreType.DMA((tokens // PATCHES,)),
            pltpu.SemaphoreType.DMA((tokens // PATCHES,)),
        ],
        compiler_params=pltpu.CompilerParams(
            collective_id=0, has_side_effects=True, vmem_limit_bytes=60 * 1024 * 1024
        ),
    )(inputs, queries, keys, values, out_weight)


def general(inputs, queries, keys, values, out_weight):
    tok_rows, local_width = queries.shape
    head_count = local_width // HEAD_DIM
    images = tok_rows // PATCHES
    split_shape = (images, PATCHES, head_count, HEAD_DIM)
    gathered = lax.all_gather(out_weight, "dp", axis=0, tiled=True)
    scores = jnp.einsum(
        "bqhd,bkhd->bhqk",
        queries.reshape(split_shape),
        keys.reshape(split_shape),
        preferred_element_type=jnp.float32,
    ) / math.sqrt(HEAD_DIM)
    row_max = jnp.max(scores, axis=-1, keepdims=True)
    shifted = jnp.exp(scores - row_max)
    probs = (shifted / jnp.sum(shifted, axis=-1, keepdims=True)).astype(jnp.bfloat16)
    attended = jnp.einsum(
        "bhqk,bkhd->bqhd", probs, values.reshape(split_shape), preferred_element_type=jnp.float32
    )
    attended = attended.astype(jnp.bfloat16).reshape(tok_rows, local_width)
    all_heads = lax.all_gather(attended, "mp", axis=1, tiled=True)
    projected = jnp.dot(all_heads, gathered, preferred_element_type=jnp.float32)
    return (inputs.astype(jnp.float32) + projected).astype(jnp.bfloat16)


def solution(mesh):
    parts, halves = mesh.shape["dp"], mesh.shape["mp"]

    def shards(inputs, queries, keys, values, out_weight):
        rows, width = out_weight.shape
        tokens = queries.shape[0]
        if (parts % 8 == 0 and 4 < parts <= 32 and halves == 2 and rows % 192 == 0 and width % 256 == 0
                and (tokens // PATCHES) * (width // HEAD_DIM) % GROUPS == 0):
            return fused(parts // 4, inputs, queries, keys, values, out_weight)
        return general(inputs, queries, keys, values, out_weight)

    return jax.shard_map(
        shards,
        mesh=mesh,
        in_specs=(P("dp", "mp"),) * 5,
        out_specs=P("dp", "mp"),
        check_vma=False,
    )
```

time: 87 us -> 78.1 us (0.90)
  Pallas kernels: 81.8 us -> 75.3 us
  local copies, waits for them, and re-layouts: 5.02 us -> 2.65 us
    pallas_call x1, Pallas kernels: 81.8 us -> 75.3 us  [fused(): pl.pallas_call(functools.partial(kernel, deep), out_shape=jax.ShapeDtypeS...]
    unnamed x7 -> x1, local copies, waits for them, and re-layouts: 5.02 us -> 2.65 us
where the time goes in v2:
time: 78.1 us; the launch traced here: 77.9 us
  Pallas kernels  75.3 us (96%)
  local copies, waits for them, and re-layouts  2.65 us (3%)
    pallas_call x1, Pallas kernels, fused(): pl.pallas_call(functools.partial(kernel, deep), out_shape=jax.ShapeDtypeS...  75.3 us
    unnamed x1, local copies, waits for them, and re-layouts  2.65 us

profile of v2, /device:TPU:0, one launch (start us, length us, event | category | flops | bytes accessed | tf_op | source)
XLA Modules:
  0.0 77.9 jit_solution(512991475129117403)
XLA Ops:
  0.0 75.3 %shard_map.55 = bf16[512,1536]{1,0:T(8,128)(2,1)} custom-call(bf16[512,1536]{1,0:T(8,128)(2,1)} %x_hbm.1, bf16[512,1536]{1,0:T(8,128)(2,1)} %q_hbm.1, bf16[512,1536]{1,0:T(8,128)(2,1)} %k_hbm.1, bf16[512,1536]{1,0:T(8,128)(2,1)} %v_hbm.1, bf16[192,1536]{1,0:T(8,128)(2,1)} %w_hbm.1), custom_call_target="tpu_custom_call" | custom-call | tf_op jit(solution)/shard_map/pallas_call | solution.py:258
  75.3 2.7 %copy.7 = bf16[512,1536]{1,0:T(8,128)(2,1)} copy(bf16[512,1536]{1,0:T(8,128)(2,1)} %shard_map.55) | data formatting | bytes 3145728

commit v3 on v2

--- a/solution.py
+++ b/solution.py
@@ -62,8 +62,8 @@
     return orders, late
 
 
-def kernel(deep, x_hbm, q_hbm, k_hbm, v_hbm, w_hbm, o_hbm,
-           wbuf, xin, qv, kv, vv, att, acc, obuf,
+def kernel(deep, x_hbm, q_hbm, k_hbm, v_hbm, w_hbm, o_ref,
+           wbuf, xin, qv, kv, vv, att, acc,
            recv, sent, local, att_sent, att_recv):
     me, half = lax.axis_index("dp"), lax.axis_index("mp")
     x, y, z = me % 2, (me // 2) % 2, me // 4
@@ -177,8 +177,7 @@
             start = xin[:, cols].astype(jnp.float32) if k == 0 else acc[:, cols]
             total = start + jnp.dot(att[:, depth], wbuf[depth, cols], preferred_element_type=jnp.float32)
             if last:
-                obuf[:, cols] = total.astype(jnp.bfloat16)
-                pltpu.make_async_copy(obuf.at[:, cols], o_hbm.at[:, cols], local.at[5 + i]).start()
+                o_ref[:, cols] = total.astype(jnp.bfloat16)
             else:
                 acc[:, cols] = total
 
@@ -245,9 +244,6 @@
         pl.when(place == at)(functools.partial(drain_all, at))
     for image in range(images):
         share(image).wait_send()
-    for i in range(width // tile):
-        cols = pl.ds(i * tile, tile)
-        pltpu.make_async_copy(obuf.at[:, cols], o_hbm.at[:, cols], local.at[5 + i]).wait()
 
 
 def fused(deep, inputs, queries, keys, values, out_weight):
@@ -257,9 +253,9 @@
     bf16, f32 = jnp.bfloat16, jnp.float32
     return pl.pallas_call(
         functools.partial(kernel, deep),
-        out_shape=jax.ShapeDtypeStruct((tokens, width), bf16),
+        out_shape=pltpu.VMEM((tokens, width), bf16),
         in_specs=[pl.BlockSpec(memory_space=pl.ANY)] * 5,
-        out_specs=pl.BlockSpec(memory_space=pl.ANY),
+        out_specs=pl.BlockSpec(memory_space=pltpu.VMEM),
         scratch_shapes=[
             pltpu.VMEM((whole, width), bf16),
             pltpu.VMEM((tokens, width), bf16),
@@ -268,15 +264,14 @@
             pltpu.VMEM((tokens, width), bf16),
             pltpu.VMEM((tokens, whole), bf16),
             pltpu.VMEM((tokens, width), f32),
-            pltpu.VMEM((tokens, width), bf16),
             pltpu.SemaphoreType.DMA((len(PARTS), 4 * deep)),
             pltpu.SemaphoreType.DMA((4,)),
-            pltpu.SemaphoreType.DMA((5 + width // 256,)),
+            pltpu.SemaphoreType.DMA((5,)),
             pltpu.SemaphoreType.DMA((tokens // PATCHES,)),
             pltpu.SemaphoreType.DMA((tokens // PATCHES,)),
         ],
         compiler_params=pltpu.CompilerParams(
-            collective_id=0, has_side_effects=True, vmem_limit_bytes=60 * 1024 * 1024
+            collective_id=0, has_side_effects=True, vmem_limit_bytes=56 * 1024 * 1024
         ),
     )(inputs, queries, keys, values, out_weight)
 

time: 78.1 us -> 75.8 us (0.971)
  local copies, waits for them, and re-layouts: 2.65 us -> 1.15 us
  Pallas kernels: 75.3 us -> 74.5 us
    unnamed x1, local copies, waits for them, and re-layouts: 2.65 us -> 1.15 us
where the time goes in v3:
time: 75.8 us; the launch traced here: 75.7 us
  Pallas kernels  74.5 us (98%)
  local copies, waits for them, and re-layouts  1.15 us (2%)
    pallas_call x1, Pallas kernels, fused(): pl.pallas_call(functools.partial(kernel, deep), out_shape=pltpu.VMEM((tok...  74.5 us

profile of v3, /device:TPU:0, one launch (start us, length us, event | category | flops | bytes accessed | tf_op | source)
XLA Modules:
  0.0 75.7 jit_solution(5219351481566898250)
XLA Ops:
  0.0 74.5 %shard_map.55 = bf16[512,1536]{1,0:T(8,128)(2,1)S(1)} custom-call(bf16[512,1536]{1,0:T(8,128)(2,1)} %x_hbm.1, bf16[512,1536]{1,0:T(8,128)(2,1)} %q_hbm.1, bf16[512,1536]{1,0:T(8,128)(2,1)} %k_hbm.1, bf16[512,1536]{1,0:T(8,128)(2,1)} %v_hbm.1, bf16[192,1536]{1,0:T(8,128)(2,1)} %w_hbm.1), custom_call_target="tpu_custom_call" | custom-call | tf_op jit(solution)/shard_map/pallas_call | solution.py:254
  74.5 1.1 %copy.7 = bf16[512,1536]{1,0:T(8,128)(2,1)} copy(bf16[512,1536]{1,0:T(8,128)(2,1)S(1)} %shard_map.55) | data formatting | bytes 3145728

commit v4 on v3

--- a/solution.py
+++ b/solution.py
@@ -14,7 +14,7 @@
 
 PARTS = (("zxy", 3), ("zyx", 3), ("xzy", 3), ("yzx", 3))
 GROUPS = 12
-HEAD_START = 4
+HEAD_START = 2
 EARLY = (1, 2)
 OWN_LATE = 0.0
 

time: 75.8 us -> 75.8 us (level)
  no operation moved by 1% of the time
where the time goes in v4:
time: 75.8 us; the launch traced here: 75.7 us
  Pallas kernels  74.5 us (98%)
  local copies, waits for them, and re-layouts  1.15 us (2%)
    pallas_call x1, Pallas kernels, fused(): pl.pallas_call(functools.partial(kernel, deep), out_shape=pltpu.VMEM((tok...  74.5 us

profile of v4, /device:TPU:0, one launch (start us, length us, event | category | flops | bytes accessed | tf_op | source)
XLA Modules:
  0.0 75.7 jit_solution(10162951150931291973)
XLA Ops:
  0.0 74.5 %shard_map.55 = bf16[512,1536]{1,0:T(8,128)(2,1)S(1)} custom-call(bf16[512,1536]{1,0:T(8,128)(2,1)} %x_hbm.1, bf16[512,1536]{1,0:T(8,128)(2,1)} %q_hbm.1, bf16[512,1536]{1,0:T(8,128)(2,1)} %k_hbm.1, bf16[512,1536]{1,0:T(8,128)(2,1)} %v_hbm.1, bf16[192,1536]{1,0:T(8,128)(2,1)} %w_hbm.1), custom_call_target="tpu_custom_call" | custom-call | tf_op jit(solution)/shard_map/pallas_call | solution.py:254
  74.5 1.1 %copy.7 = bf16[512,1536]{1,0:T(8,128)(2,1)} copy(bf16[512,1536]{1,0:T(8,128)(2,1)S(1)} %shard_map.55) | data formatting | bytes 3145728
